TPU v7x, 32 devices: a whole 2x2x4 slice. The times are simulated.
32 devices in a mesh: grp: 1, mon: 8 (over z, core), out: 4 (over y, x).
Axes of the slice: x: 2, y: 2, z: 4, core: 2. Of those that a mesh axis runs over, the one named last changes fastest.
Arguments:
- psi: float32 [2048, 512], P(('grp', 'mon', 'out')), may hold values from -6 to 6
- lodf: float32 [2048, 1024], P(('grp', 'mon'), 'out'), may hold values from -1 to 1
- block_map: int32 [16, 8], P(('grp', 'mon'), 'out'), may hold values 0 or 1
- margin: float32 [2048], P(('grp', 'mon')), may hold values from 1.5 to 4.5
- monitored: int32 [2048], P(('grp', 'mon')), may hold values from 0 to 2047, as said below
- outages: int32 [1024], P(('grp', 'out')), may hold values from 0 to 2047, as said below
Outputs:
- grad_psi: float32 [2048, 512], P(('grp', 'mon', 'out'))
Inputs may be any that keep to these rules, and one draw needn't show every extreme that they name: Branch rows are in blocks of 64; block b is owned by index (b // 4, b % 4) of (mon, out). Entries i * 256 + j * 64 to i * 256 + (j + 1) * 64 - 1 of monitored are distinct rows of block i * 4 + j. Branch 0 and branch 2048 - 1 are always among them. Entries j * 256 + i * 32 to j * 256 + (i + 1) * 32 - 1 of outages are distinct rows of block i * 4 + j, with blocks owned as for monitored. Branch 0 and branch 2048 - 1 are always among them.
All inputs are finite; a program needn't handle non-finite values. No bound on the sum of `block_map` on one device may be relied on, other than what follows from the above.
Results may differ from a plain program's by a relative error of at most 0.0001.
Values sent between devices are 32-bit elements; how exact they have to be, the bound alone decides.
A program may use at most 64 MiB of HBM per device.

v0:
```python
import jax
import jax.numpy as jnp
from jax import lax
from jax.sharding import PartitionSpec as P

BR_DEV = 64
SEL_M = 64
SEL_O = 32
LB = 128


def body(psi, lodf, block_map, margin, monitored, outages):
    width = psi.shape[1]
    mon_count = monitored.shape[0]
    out_count = outages.shape[0]
    total_out = out_count * lax.axis_size("out")
    high = lax.Precision.HIGHEST
    mon_here = lax.axis_index("mon")
    out_here = lax.axis_index("out")
    own_mon = lax.dynamic_slice_in_dim(monitored, out_here * SEL_M, SEL_M) % BR_DEV
    own_out = lax.dynamic_slice_in_dim(outages, mon_here * SEL_O, SEL_O) % BR_DEV
    own_out_rows = jnp.take(psi, own_out, axis=0)
    region_m = lax.all_gather(psi, "out", axis=0, tiled=True)
    place_m = jnp.arange(mon_count, dtype=jnp.int32) // SEL_M * BR_DEV + monitored % BR_DEV
    psi_m = jnp.take(region_m, place_m, axis=0)
    region_o = lax.all_gather(psi, "mon", axis=0, tiled=True)
    place_o = jnp.arange(out_count, dtype=jnp.int32) // SEL_O * BR_DEV + outages % BR_DEV
    psi_o = jnp.take(region_o, place_o, axis=0)
    mask_rows = block_map.astype(jnp.float32)
    eff = (
        lodf.reshape(mon_count // LB, LB, out_count // LB, LB) * mask_rows[:, None, :, None]
    ).reshape(mon_count, out_count)
    gram = (
        lax.dot_general(
            psi_m,
            psi_o,
            (((1,), (1,)), ((), ())),
            precision=high,
            preferred_element_type=jnp.float32,
        )
        / width
    )
    own_m = jnp.sum(psi_m * psi_m, axis=1) / width
    own_o = jnp.sum(psi_o * psi_o, axis=1) / width
    var = own_m[:, None] + 2.0 * eff * gram + eff * eff * own_o[None, :]
    sigma = jnp.sqrt(var + 1.0)
    weight_q = jax.nn.sigmoid(2.0 * sigma - margin[:, None]) * 2.0 / (total_out * sigma)
    weighted = weight_q * eff
    mon_part = jnp.dot(weighted, psi_o, precision=high, preferred_element_type=jnp.float32)
    mon_total, row_total = lax.psum((mon_part, jnp.sum(weight_q, axis=1)), "out")
    grad_all = row_total[:, None] * psi_m + mon_total
    grad_m = lax.dynamic_slice_in_dim(grad_all, out_here * SEL_M, SEL_M, 0)
    col_total = lax.psum(jnp.sum(weighted * eff, axis=0), "mon")
    adjoint = lax.psum_scatter(
        lax.dot_general(
            weighted,
            psi_m,
            (((0,), (0,)), ((), ())),
            precision=high,
            preferred_element_type=jnp.float32,
        ),
        "mon",
        scatter_dimension=0,
        tiled=True,
    )
    own_col = lax.dynamic_slice_in_dim(col_total, mon_here * SEL_O, SEL_O)
    grad_o = adjoint + own_col[:, None] * own_out_rows
    grad_psi = jnp.zeros(psi.shape, jnp.float32).at[own_mon].add(grad_m).at[own_out].add(grad_o)
    return grad_psi


def solution(mesh):
    in_specs = (
        P(("grp", "mon", "out"), None),
        P(("grp", "mon"), "out"),
        P(("grp", "mon"), "out"),
        P(("grp", "mon")),
        P(("grp", "mon")),
        P(("grp", "out")),
    )
    out_specs = P(("grp", "mon", "out"), None)
    return jax.shard_map(body, mesh=mesh, in_specs=in_specs, out_specs=out_specs, check_vma=False)
```

profile of v0, /device:TPU:0, one launch (start us, length us, event | category | flops | bytes accessed | tf_op | source)
XLA Modules:
  0.0 127.4 jit_solution(10508152473319571866)
XLA Ops:
  6.5 0.0 all-gather.2.cloned.1.call-start
  6.5 0.7 all-gather.2.cloned.1.call-update
  7.3 0.0 all-reduce.2.cloned.1.call-start
  7.3 0.1 copy-done
  7.5 11.6 %all_gather.6 = f32[256,512]{1,0:T(8,128)S(1)} all-gather(f32[64,512]{1,0:T(8,128)S(1)} %copy-done), channel_id=1, replica_groups=mesh['grp'=1,'mon'=8,'out'=4] {'out'}, dimensions={0}, use_global_device_ids=true | all-gather | bytes 655360 | tf_op jit(solution)/shard_map/all_gather | solution.py:23
  19.1 0.0 copy-start.2
  19.1 1.0 gather_fusion
  20.1 0.2 multiply_reduce_fusion.1
  20.3 0.0 copy-start.1
  20.4 0.1 mul.85
  20.5 0.8 copy-done.1
  21.3 12.5 %all-gather.2.cloned.1.call-done = f32[512,512]{1,0:T(8,128)} async-done(((f32[64,512]{1,0:T(8,128)}), f32[512,512]{1,0:T(8,128)}) %all-gather.2.cloned.1.call-update) | async-done | bytes 1048592 | tf_op jit(solution)/shard_map/all_gather | solution.py:26
  33.8 2.4 %gather_fusion.1 = f32[256,512]{1,0:T(8,128)S(1)} fusion(f32[512,512]{1,0:T(8,128)} %all-gather.2.cloned.1.call-done, s32[1024]{0:T(1024)S(1)} %pad_clamp_fusion.1), kind=kCustom, calls=%fused_computation.1 | custom fusion | bytes 1049600 | tf_op jit(solution)/shard_map/jit(_take)/gather | solution.py:28
  36.2 0.2 multiply_reduce_fusion
  36.4 0.0 copy-start.5
  36.5 0.7 copy-done.5
  37.1 1.0 multiply_reduce_fusion.2
  38.1 1.6 %fusion.5 = f32[256,512]{1,0:T(8,128)} fusion(f32[256,512]{1,0:T(8,128)S(1)} %gather_fusion.1, pred[256]{0:T(512)(128)(4,1)S(1)} %get-tuple-element.13, f32[256,256]{1,0:T(8,128)S(1)} %get-tuple-element.15, f32[256,256]{1,0:T(8,128)S(1)} %bitcast_multiply_fusion), kind=kOutput, calls=%fused_computation.13 | convolution fusion | flops 402849792 | bytes 1573120 | tf_op jit(solution)/shard_map/dot_general | solution.py:49
  39.7 0.0 all-reduce.2.cloned.1.call-update
  39.7 0.0 reduce-scatter.2.cloned.1.call-start
  39.8 1.5 %fusion.15 = f32[256,512]{1,0:T(8,128)} fusion(f32[256,512]{1,0:T(8,128)S(1)} %get-tuple-element.10, f32[256,256]{1,0:T(8,128)S(1)} %get-tuple-element.15, f32[256,256]{1,0:T(8,128)S(1)} %bitcast_multiply_fusion), kind=kOutput, calls=%fused_computation.27 | convolution fusion | flops 402718720 | bytes 1572864 | tf_op jit(solution)/shard_map/dot_general | solution.py:55
  41.2 0.0 reduce-scatter.2.cloned.1.call-update
  41.3 0.1 compare_select_fusion.3
  41.4 0.1 compare_and_fusion
  41.4 9.9 %psum.21 = f32[256]{0:T(256)S(1)} all-reduce(f32[256]{0:T(256)S(1)} %get-tuple-element.6), channel_id=1, replica_groups=mesh['grp'=1,'mon'=8,'out'=4] {'out'}, use_global_device_ids=true, to_apply=%region_3.4 | all-reduce | flops 256 | bytes 2048 | tf_op jit(solution)/shard_map/psum | solution.py:50
  51.4 0.1 dynamic-slice
  51.5 13.6 %psum.23 = f32[256]{0:T(256)S(1)} all-reduce(f32[256]{0:T(256)S(1)} %get-tuple-element.5), channel_id=1, replica_groups=mesh['grp'=1,'mon'=8,'out'=4] {'mon'}, use_global_device_ids=true, to_apply=%region_8.9 | all-reduce | flops 256 | bytes 2048 | tf_op jit(solution)/shard_map/psum | solution.py:53
  65.0 0.1 dynamic_slice.15
  65.1 19.8 %all-reduce.2.cloned.1.call-done = f32[256,512]{1,0:T(8,128)} async-done(((f32[256,512]{1,0:T(8,128)}), f32[256,512]{1,0:T(8,128)}) %all-reduce.2.cloned.1.call-update) | async-done | bytes 524304 | tf_op jit(solution)/shard_map/psum | solution.py:50
  84.9 2.0 %scatter_custom_fusion = f32[64,512]{1,0:T(8,128)} fusion(s32[64]{0:T(128)S(1)} %compare_select_fusion.3, f32[256,512]{1,0:T(8,128)} %all-reduce.2.cloned.1.call-done, s32[]{:T(128)S(6)} %select_n.68, s32[]{:T(128)} %constant.118.clone.1, f32[256,512]{1,0:T(8,128)S(1)} %get-tuple-element.10, f32[64]{0:T(128)S(1)} %dynamic-slice, f32[]{:T(128)} %constant.115.clone.1), kind=kCustom, calls=%fused_computation.25 | custom fusion | flops 98304 | bytes 394756 | tf_op jit(solution)/shard_map/scatter-add | solution.py:68
  86.9 31.2 %reduce-scatter.2.cloned.1.call-done = f32[32,512]{1,0:T(8,128)} async-done(((f32[256,512]{1,0:T(8,128)}), f32[32,512]{1,0:T(8,128)}) %reduce-scatter.2.cloned.1.call-update) | async-done | bytes 65552 | tf_op jit(solution)/shard_map/reduce_scatter | solution.py:54
  118.1 2.7 %scatter_custom_fusion.1 = f32[64,512]{1,0:T(8,128)} fusion(f32[64,512]{1,0:T(8,128)} %scatter_custom_fusion, s32[32]{0:T(128)S(1)} %get-tuple-element.8, f32[32,512]{1,0:T(8,128)} %reduce-scatter.2.cloned.1.call-done, f32[]{:T(128)} %constant.126.clone.1, f32[32]{0:T(128)S(1)} %dynamic_slice.15, pred[32]{0:T(512)(128)(4,1)S(1)} %get-tuple-element.7, ...), kind=kCustom, calls=%fused_computation.31 | custom fusion | flops 65536 | bytes 333312 | tf_op jit(solution)/shard_map/scatter-add | solution.py:68
  (15 shorter events, 0.1 us)
Async XLA Ops:
  6.5 0.9 copy-start
  6.5 0.8 copy-start.3
  6.5 27.3 %all-gather.2.cloned.1.call-start = ((), (), s32[]{:S(2)}) async-start(), calls=%async_computation.1 | async-start | bytes 1179648 | tf_op jit(solution)/shard_map/all_gather | solution.py:26
  7.3 77.6 %all-reduce.2.cloned.1.call-start = ((), (), s32[]{:S(2)}) async-start(), calls=%async_computation.2 | async-start | bytes 1048576 | tf_op jit(solution)/shard_map/psum | solution.py:50
  7.5 11.6 %copy-start.4 = (s32[256]{0:T(256)S(1)}, s32[256]{0:T(256)}, u32[]{:S(2)}) copy-start(s32[256]{0:T(256)} %param.10) | copy-start | bytes 3076
  19.1 1.0 copy-start.2
  20.3 1.0 copy-start.1
  36.4 0.7 copy-start.5
  39.7 78.4 %reduce-scatter.2.cloned.1.call-start = ((), (), s32[]{:S(2)}) async-start(), calls=%async_computation.3 | async-start | bytes 589824 | tf_op jit(solution)/shard_map/reduce_scatter | solution.py:54
Sparse Core Ops, SparseCore 0:
  9.0 24.7 all-gather.1
  39.8 45.0 all-reduce.1
  87.2 30.9 reduce-scatter.1
where the time goes:
time: 128 us; the launch traced here: 127 us
  waiting for transfers between devices  64.2 us (50%)
  blocking collectives  35.1 us (27%)
  between operations  13.2 us (10%)
  other arithmetic  5.39 us (4%)
  local copies, waits for them, and re-layouts  5.31 us (4%)
  matrix products  4.03 us (3%)
    reduce_scatter x1, waiting for transfers between devices, body(): lax.psum_scatter(lax.dot_general(weighted, psi_m, (((0,), (0,)), ((), ())...  31.2 us
    psum x1, waiting for transfers between devices, body(): lax.psum((mon_part, jnp.sum(weight_q, axis=1)), 'out')  19.8 us
    psum x1, blocking collectives, body(): col_total = lax.psum(jnp.sum(weighted * eff, axis=0), 'mon')  13.6 us
    all_gather x1, waiting for transfers between devices, body(): region_o = lax.all_gather(psi, 'mon', axis=0, tiled=True)  12.5 us
    all_gather x1, blocking collectives, body(): region_m = lax.all_gather(psi, 'out', axis=0, tiled=True)  11.6 us
    psum x1, blocking collectives, body(): lax.psum((mon_part, jnp.sum(weight_q, axis=1)), 'out')  9.93 us
    scatter-add x2, other arithmetic, body(): jnp.zeros(psi.shape, jnp.float32).at[own_mon].add(grad_m).at[own_out]  4.71 us
  transfers between devices with their start and end apart: 3, of which 3 were waited for; matrix products, arithmetic and copies ran while one was open for 4% of the time, Pallas kernels for 0%

commit v1 on v0

v1 whole, which is shorter than its diff:
```python
import functools

import jax
import jax.numpy as jnp
from jax import lax
from jax.experimental import pallas as pl
from jax.experimental.pallas import tpu as pltpu
from jax.sharding import PartitionSpec as P

BR_DEV = 64
SEL_M = 64
SEL_O = 32
LB = 128
OC = 256
MESH = pl.DeviceIdType.MESH
F32 = jnp.float32
BF16 = jnp.bfloat16


def split(a):
    hi = a.astype(BF16)
    return hi, (a - hi.astype(F32)).astype(BF16)


def dot3(a, b, dims):
    dn = (dims, ((), ()))
    dot = functools.partial(lax.dot_general, dimension_numbers=dn, preferred_element_type=F32)
    return dot(a[0], b[0]) + (dot(a[0], b[1]) + dot(a[1], b[0]))


def kernel(n_mon, n_out, scale,
           psi_hbm, lodf_ref, map_ref, margin_ref, mon_ref, outs_ref,
           out_ref,
           pv, pm, po, sel, selt, eff, marg, mpart, adj, rm, rs, rz,
           loc_sem, sm_s, sm_r, so_s, so_r, fw_s, rl_s, bm_s, bm_r, bs_s, bs_r, bz_s, bz_r):
    nz = n_mon // 2
    i = lax.axis_index("mon")
    j = lax.axis_index("out")
    z = i // 2
    c = lax.rem(i, 2)
    sib = i + 1 - 2 * c
    width = pm.shape[2]
    mon_count = n_out * SEL_M
    out_count = n_mon * SEL_O
    per = OC // SEL_O
    chunks = out_count // OC

    def to_out(d):
        return lax.rem(j + d, n_out)

    def from_out(d):
        return lax.rem(j + n_out - d, n_out)

    def to_z(d):
        return lax.rem(z + d, nz)

    def from_z(d):
        return lax.rem(z + nz - d, nz)

    def loop(count, f):
        if count <= 8:
            for d in range(count):
                f(d)
        else:
            lax.fori_loop(0, count, lambda d, x: (f(d), x)[1], 0)

    load = pltpu.make_async_copy(psi_hbm, pv, loc_sem)
    load.start()
    barrier = pltpu.get_barrier_semaphore()

    def sig_out(d):
        pl.semaphore_signal(barrier, inc=1, device_id={"out": to_out(d + 1)}, device_id_type=MESH)

    def sig_z(d):
        pl.semaphore_signal(barrier, inc=1, device_id={"mon": 2 * to_z(d + 1) + c}, device_id_type=MESH)

    loop(n_out - 1, sig_out)
    loop(nz - 1, sig_z)
    pl.semaphore_signal(barrier, inc=1, device_id={"mon": sib}, device_id_type=MESH)
    load.wait()
    for k in range(SEL_O):
        row = lax.rem(outs_ref[i * SEL_O + k], BR_DEV)
        sel[pl.ds(k, 1), :] = pv[pl.ds(row, 1), :]
    pl.semaphore_wait(barrier, n_out - 1 + nz - 1 + 1)

    def copy_m(d):
        return pltpu.make_async_remote_copy(
            pv, pm.at[j], sm_s.at[d], sm_r.at[j],
            device_id={"out": to_out(d + 1)}, device_id_type=MESH)

    def recv_m(d):
        s = from_out(d + 1)
        return pltpu.make_async_remote_copy(
            pv, pm.at[s], sm_s.at[d], sm_r.at[s],
            device_id={"out": to_out(d + 1)}, device_id_type=MESH)

    def copy_o(d):
        return pltpu.make_async_remote_copy(
            sel, po.at[i], so_s.at[d], so_r.at[i],
            device_id={"mon": 2 * to_z(d + 1) + c}, device_id_type=MESH)

    def copy_s():
        return pltpu.make_async_remote_copy(
            sel, po.at[i], fw_s, so_r.at[i],
            device_id={"mon": sib}, device_id_type=MESH)

    def from_slot(slot):
        return pltpu.make_async_remote_copy(
            sel, po.at[slot], fw_s, so_r.at[slot],
            device_id={"mon": sib}, device_id_type=MESH)

    def relay(d):
        slot = 2 * from_z(d + 1) + c
        return pltpu.make_async_remote_copy(
            po.at[slot], po.at[slot], rl_s.at[d], so_r.at[slot],
            device_id={"mon": sib}, device_id_type=MESH)

    loop(nz - 1, lambda d: copy_o(d).start())
    loop(n_out - 1, lambda d: copy_m(d).start())
    copy_s().start()
    po[i] = sel[...]
    pm[j] = pv[...]

    lane = lax.broadcasted_iota(jnp.int32, (1, BR_DEV), 1)
    for k in range(SEL_O):
        row = lax.rem(outs_ref[i * SEL_O + k], BR_DEV)
        selt[pl.ds(k, 1), :] = (lane == row).astype(F32)
    col = lax.broadcasted_iota(jnp.int32, (1, mon_count), 1)
    place = col // SEL_M * BR_DEV + lax.rem(mon_ref[...], BR_DEV)
    hit = lax.broadcasted_iota(jnp.int32, (mon_count, mon_count), 0) == place
    marg[...] = jnp.sum(jnp.where(hit, margin_ref[...], 0.0), axis=1, keepdims=True)
    perm = hit.astype(BF16)

    def lay(ch, _):
        if chunks == 1:
            cols = slice(0, OC)
        else:
            cols = pl.ds(pl.multiple_of(ch * OC, OC), OC)
        lf = lodf_ref[:, cols]
        parts = []
        for a in range(mon_count // LB):
            parts.append(jnp.concatenate(
                [lf[a * LB:(a + 1) * LB, b * LB:(b + 1) * LB] * map_ref[a, ch * (OC // LB) + b].astype(F32)
                 for b in range(OC // LB)], axis=1))
        e = jnp.concatenate(parts, axis=0)
        e0 = e.astype(BF16)
        r1 = e - e0.astype(F32)
        e1 = r1.astype(BF16)
        e2 = (r1 - e1.astype(F32)).astype(BF16)
        dot = functools.partial(jnp.dot, preferred_element_type=F32)
        eff[:, cols] = dot(perm, e0) + (dot(perm, e1) + dot(perm, e2))
        return 0

    if chunks == 1:
        lay(0, 0)
    else:
        lax.fori_loop(0, chunks, lay, 0)

    def take_z(d):
        slot = 2 * from_z(d + 1) + c
        from_slot(slot).wait_recv()
        relay(d).start()

    loop(nz - 1, take_z)
    loop(n_out - 1, lambda d: recv_m(d).wait_recv())
    from_slot(sib).wait_recv()
    loop(nz - 1, lambda d: from_slot(2 * from_z(d + 1) + 1 - c).wait_recv())

    psi_m = pm[...].reshape(mon_count, width)
    m2 = split(psi_m)
    own_m = jnp.sum(psi_m * psi_m, axis=1, keepdims=True) * (1.0 / width)
    margin = marg[...]
    ones_o = jnp.ones((8, width), BF16)
    ones_m = jnp.ones((mon_count, 128), BF16)

    def compute(ch, _):
        if chunks == 1:
            cols = slice(0, OC)
            rows = slice(0, per)
        else:
            cols = pl.ds(pl.multiple_of(ch * OC, OC), OC)
            rows = pl.ds(ch * per, per)
        psi_o = po[rows].reshape(OC, width)
        o2 = split(psi_o)
        gram = dot3(m2, o2, ((1,), (1,))) * (1.0 / width)
        s2 = split(psi_o * psi_o)
        dn = (((1,), (1,)), ((), ()))
        own_o = (lax.dot_general(ones_o, s2[0], dn, preferred_element_type=F32)
                 + lax.dot_general(ones_o, s2[1], dn, preferred_element_type=F32))[0:1] * (1.0 / width)
        e = eff[:, cols]
        var1 = (own_m + 1.0) + e * (2.0 * gram + e * own_o)
        inv = lax.rsqrt(var1)
        q = inv * scale / (1.0 + jnp.exp(margin - 2.0 * (var1 * inv)))
        w = q * e
        w2 = split(w)
        part = dot3(w2, o2, ((1,), (0,))) + jnp.sum(q, axis=1, keepdims=True) * psi_m
        part = part.reshape(n_out, SEL_M, width)
        if chunks == 1:
            mpart[...] = part
        else:
            @pl.when(ch == 0)
            def _():
                mpart[...] = part

            @pl.when(ch > 0)
            def _():
                mpart[...] += part
        c2 = split(w * e)
        dn0 = (((0,), (0,)), ((), ()))
        colsum = (lax.dot_general(c2[0], ones_m, dn0, preferred_element_type=F32)
                  + lax.dot_general(c2[1], ones_m, dn0, preferred_element_type=F32))[:, 0:1]
        a = dot3(w2, m2, ((0,), (0,))) + colsum * psi_o
        a = a.reshape(per, SEL_O, width)
        for b in range(per):
            adj[b % 2, ch * (per // 2) + b // 2] = a[b]
        return 0

    if chunks == 1:
        compute(0, 0)
    else:
        lax.fori_loop(0, chunks, compute, 0)

    def sib_copy(d):
        zz = to_z(d)
        return pltpu.make_async_remote_copy(
            adj.at[1 - c, zz], rs.at[zz], bs_s.at[zz], bs_r.at[zz],
            device_id={"mon": sib}, device_id_type=MESH)

    def z_copy(d):
        zz = to_z(d)
        return pltpu.make_async_remote_copy(
            adj.at[c, zz], rz.at[z], bz_s.at[d], bz_r.at[z],
            device_id={"mon": 2 * zz + c}, device_id_type=MESH)

    def z_recv(d):
        zz = from_z(d)
        return pltpu.make_async_remote_copy(
            adj.at[c, zz], rz.at[zz], bz_s.at[d], bz_r.at[zz],
            device_id={"mon": 2 * zz + c}, device_id_type=MESH)

    def b_copy(d):
        p = to_out(d + 1)
        return pltpu.make_async_remote_copy(
            mpart.at[p], rm.at[j], bm_s.at[d], bm_r.at[j],
            device_id={"out": p}, device_id_type=MESH)

    def b_recv(d):
        s = from_out(d + 1)
        return pltpu.make_async_remote_copy(
            mpart.at[s], rm.at[s], bm_s.at[d], bm_r.at[s],
            device_id={"out": s}, device_id_type=MESH)

    loop(nz, lambda d: sib_copy((d + 1) % nz if isinstance(d, int) else lax.rem(d + 1, nz)).start())
    loop(n_out - 1, lambda d: b_copy(d).start())

    def pass_z(d):
        zz = to_z(d + 1)
        sib_copy(d + 1).wait_recv()
        adj[c, zz] = adj[c, zz] + rs[zz]
        z_copy(d + 1).start()

    loop(nz - 1, pass_z)
    sib_copy(0).wait_recv()
    rz[z] = adj[c, z] + rs[z]

    loop(nz - 1, lambda d: z_recv(d + 1).wait_recv())
    if nz <= 8:
        tot = rz[z]
        for d in range(1, nz):
            tot = tot + rz[from_z(d)]
    else:
        tot = lax.fori_loop(1, nz, lambda d, t: t + rz[from_z(d)], rz[z])
    t0 = tot.astype(BF16)
    r1 = tot - t0.astype(F32)
    t1 = r1.astype(BF16)
    t2 = (r1 - t1.astype(F32)).astype(BF16)
    st = selt[...].astype(BF16)
    dn0 = (((0,), (0,)), ((), ()))
    put = functools.partial(lax.dot_general, dimension_numbers=dn0, preferred_element_type=F32)
    res = put(st, t0) + (put(st, t1) + put(st, t2)) + mpart[j]
    for d in range(n_out - 1):
        b_recv(d).wait_recv()
        res = res + rm[from_out(d + 1)]
    out_ref[...] = res

    loop(nz - 1, lambda d: copy_o(d).wait_send())
    loop(n_out - 1, lambda d: copy_m(d).wait_send())
    copy_s().wait_send()
    loop(nz - 1, lambda d: relay(d).wait_send())
    loop(nz, lambda d: sib_copy(d).wait_send())
    loop(nz - 1, lambda d: z_copy(d + 1).wait_send())
    loop(n_out - 1, lambda d: b_copy(d).wait_send())


def body(n_mon, n_out, psi, lodf, block_map, margin, monitored, outages):
    width = psi.shape[1]
    mon_count = monitored.shape[0]
    out_count = outages.shape[0]
    nz = n_mon // 2
    total_out = out_count * n_out
    vm = pl.BlockSpec(memory_space=pltpu.VMEM)
    sm = pl.BlockSpec(memory_space=pltpu.SMEM)
    dma = pltpu.SemaphoreType.DMA
    return pl.pallas_call(
        functools.partial(kernel, n_mon, n_out, 2.0 / total_out),
        out_shape=jax.ShapeDtypeStruct(psi.shape, F32),
        in_specs=[pl.BlockSpec(memory_space=pl.ANY), vm, sm, vm, vm, sm],
        out_specs=vm,
        scratch_shapes=[
            pltpu.VMEM(psi.shape, F32),
            pltpu.VMEM((n_out, BR_DEV, width), F32),
            pltpu.VMEM((n_mon, SEL_O, width), F32),
            pltpu.VMEM((SEL_O, width), F32),
            pltpu.VMEM((SEL_O, BR_DEV), F32),
            pltpu.VMEM((mon_count, out_count), F32),
            pltpu.VMEM((mon_count, 1), F32),
            pltpu.VMEM((n_out, BR_DEV, width), F32),
            pltpu.VMEM((2, nz, SEL_O, width), F32),
            pltpu.VMEM((n_out, BR_DEV, width), F32),
            pltpu.VMEM((nz, SEL_O, width), F32),
            pltpu.VMEM((nz, SEL_O, width), F32),
            dma(()), dma((n_out - 1,)), dma((n_out,)), dma((nz,)), dma((n_mon,)),
            dma(()), dma((nz,)), dma((n_out - 1,)), dma((n_out,)),
            dma((nz,)), dma((nz,)), dma((nz,)), dma((nz,)),
        ],
        compiler_params=pltpu.CompilerParams(
            collective_id=0, has_side_effects=True, vmem_limit_bytes=40 << 20),
        name="flow_variance_grad",
    )(psi, lodf, block_map, margin.reshape(1, -1), monitored.reshape(1, -1), outages)


def solution(mesh):
    in_specs = (
        P(("grp", "mon", "out"), None),
        P(("grp", "mon"), "out"),
        P(("grp", "mon"), "out"),
        P(("grp", "mon")),
        P(("grp", "mon")),
        P(("grp", "out")),
    )
    out_specs = P(("grp", "mon", "out"), None)
    fn = functools.partial(body, mesh.shape["mon"], mesh.shape["out"])
    return jax.shard_map(fn, mesh=mesh, in_specs=in_specs, out_specs=out_specs, check_vma=False)
```

time: 128 us -> 27.2 us (0.21)
  waiting for transfers between devices: 64.2 us -> 0 us
  blocking collectives: 35.1 us -> 0 us
  Pallas kernels: 0 us -> 23.1 us
  between operations: 13.2 us -> 0.02 us
  other arithmetic: 5.39 us -> 0 us
  matrix products: 4.03 us -> 0 us
  local copies, waits for them, and re-layouts: 5.31 us -> 3.9 us
    reduce_scatter x1 -> x0, waiting for transfers between devices: 31.2 us -> none  [body(): lax.psum_scatter(lax.dot_general(weighted, psi_m, (((0,), (0,)), ((), ())...]
    psum x2 -> x0, blocking collectives: 23.5 us -> none  [the longest x1 13.6 us: body(): col_total = lax.psum(jnp.sum(weighted * eff, axis=0), 'mon')]
    pallas_call x0 -> x1, Pallas kernels: none -> 23.1 us  [body(): pl.pallas_call(functools.partial(kernel, n_mon, n_out, 2.0 / total_out),...]
    psum x1 -> x0, waiting for transfers between devices: 19.8 us -> none  [body(): lax.psum((mon_part, jnp.sum(weight_q, axis=1)), 'out')]
    all_gather x1 -> x0, waiting for transfers between devices: 12.5 us -> none  [body(): region_o = lax.all_gather(psi, 'mon', axis=0, tiled=True)]
    all_gather x1 -> x0, blocking collectives: 11.6 us -> none  [body(): region_m = lax.all_gather(psi, 'out', axis=0, tiled=True)]
    scatter-add x2 -> x0, other arithmetic: 4.71 us -> none  [body(): jnp.zeros(psi.shape, jnp.float32).at[own_mon].add(grad_m).at[own_out]]
    dot_general x3 -> x0, matrix products: 4.03 us -> none  [the longest x1 1.55 us: body(): jnp.dot(weighted, psi_o, precision=high, preferred_element_type=jnp.float32)]
  transfers between devices with their start and end apart: 3 -> 0, of which waited for: 3 -> 0; matrix products, arithmetic and copies ran while one was open for 4% -> 0% of each run, Pallas kernels for 0% -> 0%
where the time goes in v1:
time: 27.2 us; the launch traced here: 27 us
  Pallas kernels  23.1 us (85%)
  local copies, waits for them, and re-layouts  3.9 us (14%)
    pallas_call x1, Pallas kernels, body(): pl.pallas_call(functools.partial(kernel, n_mon, n_out, 2.0 / total_out),...  23.1 us
    unnamed x13, local copies, waits for them, and re-layouts  3.9 us

profile of v1, /device:TPU:0, one launch (start us, length us, event | category | flops | bytes accessed | tf_op | source)
XLA Modules:
  0.0 27.0 jit_solution(12508889551294336692)
XLA Ops:
  0.0 0.0 copy-start.3
  0.0 0.0 copy-start.4
  0.0 0.0 copy-start.2
  0.0 0.7 %copy-done.3 = f32[256]{0:T(256)S(1)} copy-done((f32[256]{0:T(256)S(1)}, f32[256]{0:T(256)}, u32[]{:S(2)}) %copy-start.3) | copy-done | bytes 1048
  0.7 0.0 copy-done.4
  0.7 0.0 copy-done.2
  0.7 0.0 copy-start
  0.7 0.9 %copy-done = f32[256,256]{1,0:T(8,128)S(1)} copy-done((f32[256,256]{1,0:T(8,128)S(1)}, f32[256,256]{1,0:T(8,128)}, u32[]{:S(2)}) %copy-start) | copy-done | bytes 262168
  1.7 0.0 copy-start.1
  1.7 0.9 %copy-done.1 = f32[64,512]{1,0:T(8,128)S(1)} copy-done((f32[64,512]{1,0:T(8,128)S(1)}, f32[64,512]{1,0:T(8,128)}, u32[]{:S(2)}) %copy-start.1) | copy-done | bytes 131096
  2.6 0.0 copy-start.5
  2.6 0.7 %copy-done.5 = s32[256]{0:T(256)S(1)} copy-done((s32[256]{0:T(256)S(1)}, s32[256]{0:T(256)}, u32[]{:S(2)}) %copy-start.5) | copy-done | bytes 1048
  3.2 23.1 %flow_variance_grad.1 = f32[64,512]{1,0:T(8,128)S(1)} custom-call(f32[64,512]{1,0:T(8,128)S(1)} %copy-done.1, f32[256,256]{1,0:T(8,128)S(1)} %copy-done, s32[2,2]{1,0:T(2,128)S(1)} %copy-done.2, f32[1,256]{1,0:T(1,128)S(1)} %bitcast.2, s32[1,256]{1,0:T(1,128)S(1)} %bitcast.3, s32[256]{0:T(256)S(1)} %copy-done.5), custom_call_target="tpu_custom_call" | custom-call | tf_op jit(solution)/shard_map/flow_variance_grad/pallas_call | solution.py:304
  26.3 0.7 %copy.8 = f32[64,512]{1,0:T(8,128)} copy(f32[64,512]{1,0:T(8,128)S(1)} %flow_variance_grad.1) | data formatting | bytes 262144
Async XLA Ops:
  0.0 0.7 %copy-start.3 = (f32[256]{0:T(256)S(1)}, f32[256]{0:T(256)}, u32[]{:S(2)}) copy-start(f32[256]{0:T(256)} %param.9) | copy-start | bytes 3076
  0.0 0.7 %copy-start.4 = (s32[256]{0:T(256)S(1)}, s32[256]{0:T(256)}, u32[]{:S(2)}) copy-start(s32[256]{0:T(256)} %param.10) | copy-start | bytes 3076
  0.0 0.7 %copy-start.2 = (s32[2,2]{1,0:T(2,128)S(1)}, s32[2,2]{1,0:T(2,128)}, u32[]{:S(2)}) copy-start(s32[2,2]{1,0:T(2,128)} %map_ref.1) | copy-start | bytes 52
  0.7 0.9 %copy-start = (f32[256,256]{1,0:T(8,128)S(1)}, f32[256,256]{1,0:T(8,128)}, u32[]{:S(2)}) copy-start(f32[256,256]{1,0:T(8,128)} %lodf_ref.1) | copy-start | bytes 786436
  1.7 0.9 %copy-start.1 = (f32[64,512]{1,0:T(8,128)S(1)}, f32[64,512]{1,0:T(8,128)}, u32[]{:S(2)}) copy-start(f32[64,512]{1,0:T(8,128)} %psi_hbm.1) | copy-start | bytes 393220
  2.6 0.7 %copy-start.5 = (s32[256]{0:T(256)S(1)}, s32[256]{0:T(256)}, u32[]{:S(2)}) copy-start(s32[256]{0:T(256)} %outs_ref.1) | copy-start | bytes 3076

commit v2 on v1

--- a/solution.py
+++ b/solution.py
@@ -29,8 +29,9 @@
 
 
 def kernel(n_mon, n_out, scale,
-           psi_hbm, lodf_ref, map_ref, margin_ref, mon_ref, outs_ref,
+           psi_hbm, lodf_hbm, map_hbm, margin_hbm, mon_hbm, outs_hbm,
            out_ref,
+           lodf_ref, map_ref, margin_ref, mon_ref, outs_ref,
            pv, pm, po, sel, selt, eff, marg, mpart, adj, rm, rs, rz,
            loc_sem, sm_s, sm_r, so_s, so_r, fw_s, rl_s, bm_s, bm_r, bs_s, bs_r, bz_s, bz_r):
     nz = n_mon // 2
@@ -64,8 +65,11 @@
         else:
             lax.fori_loop(0, count, lambda d, x: (f(d), x)[1], 0)
 
-    load = pltpu.make_async_copy(psi_hbm, pv, loc_sem)
-    load.start()
+    loads = [pltpu.make_async_copy(a, b, loc_sem.at[k]) for k, (a, b) in enumerate([
+        (outs_hbm, outs_ref), (psi_hbm, pv), (mon_hbm, mon_ref),
+        (margin_hbm, margin_ref), (map_hbm, map_ref), (lodf_hbm, lodf_ref)])]
+    for load in loads:
+        load.start()
     barrier = pltpu.get_barrier_semaphore()
 
     def sig_out(d):
@@ -77,7 +81,8 @@
     loop(n_out - 1, sig_out)
     loop(nz - 1, sig_z)
     pl.semaphore_signal(barrier, inc=1, device_id={"mon": sib}, device_id_type=MESH)
-    load.wait()
+    loads[0].wait()
+    loads[1].wait()
     for k in range(SEL_O):
         row = lax.rem(outs_ref[i * SEL_O + k], BR_DEV)
         sel[pl.ds(k, 1), :] = pv[pl.ds(row, 1), :]
@@ -125,6 +130,8 @@
     for k in range(SEL_O):
         row = lax.rem(outs_ref[i * SEL_O + k], BR_DEV)
         selt[pl.ds(k, 1), :] = (lane == row).astype(F32)
+    for load in loads[2:]:
+        load.wait()
     col = lax.broadcasted_iota(jnp.int32, (1, mon_count), 1)
     place = col // SEL_M * BR_DEV + lax.rem(mon_ref[...], BR_DEV)
     hit = lax.broadcasted_iota(jnp.int32, (mon_count, mon_count), 0) == place
@@ -299,14 +306,18 @@
     nz = n_mon // 2
     total_out = out_count * n_out
     vm = pl.BlockSpec(memory_space=pltpu.VMEM)
-    sm = pl.BlockSpec(memory_space=pltpu.SMEM)
     dma = pltpu.SemaphoreType.DMA
     return pl.pallas_call(
         functools.partial(kernel, n_mon, n_out, 2.0 / total_out),
         out_shape=jax.ShapeDtypeStruct(psi.shape, F32),
-        in_specs=[pl.BlockSpec(memory_space=pl.ANY), vm, sm, vm, vm, sm],
+        in_specs=[pl.BlockSpec(memory_space=pl.ANY)] * 6,
         out_specs=vm,
         scratch_shapes=[
+            pltpu.VMEM(lodf.shape, F32),
+            pltpu.SMEM(block_map.shape, jnp.int32),
+            pltpu.VMEM((1, mon_count), F32),
+            pltpu.VMEM((1, mon_count), jnp.int32),
+            pltpu.SMEM(outages.shape, jnp.int32),
             pltpu.VMEM(psi.shape, F32),
             pltpu.VMEM((n_out, BR_DEV, width), F32),
             pltpu.VMEM((n_mon, SEL_O, width), F32),
@@ -319,12 +330,12 @@
             pltpu.VMEM((n_out, BR_DEV, width), F32),
             pltpu.VMEM((nz, SEL_O, width), F32),
             pltpu.VMEM((nz, SEL_O, width), F32),
-            dma(()), dma((n_out - 1,)), dma((n_out,)), dma((nz,)), dma((n_mon,)),
+            dma((6,)), dma((n_out - 1,)), dma((n_out,)), dma((nz,)), dma((n_mon,)),
             dma(()), dma((nz,)), dma((n_out - 1,)), dma((n_out,)),
             dma((nz,)), dma((nz,)), dma((nz,)), dma((nz,)),
         ],
         compiler_params=pltpu.CompilerParams(
-            collective_id=0, has_side_effects=True, vmem_limit_bytes=40 << 20),
+            collective_id=0, has_side_effects=True, vmem_limit_bytes=60 << 20),
         name="flow_variance_grad",
     )(psi, lodf, block_map, margin.reshape(1, -1), monitored.reshape(1, -1), outages)
 

time: 27.2 us -> 24.7 us (0.908)
  local copies, waits for them, and re-layouts: 3.9 us -> 1.57 us
    unnamed x13 -> x1, local copies, waits for them, and re-layouts: 3.9 us -> 1.57 us
where the time goes in v2:
time: 24.7 us; the launch traced here: 24.6 us
  Pallas kernels  23 us (93%)
  local copies, waits for them, and re-layouts  1.57 us (6%)
    pallas_call x1, Pallas kernels, body(): pl.pallas_call(functools.partial(kernel, n_mon, n_out, 2.0 / total_out),...  23 us
    unnamed x1, local copies, waits for them, and re-layouts  1.57 us

profile of v2, /device:TPU:0, one launch (start us, length us, event | category | flops | bytes accessed | tf_op | source)
XLA Modules:
  0.0 24.6 jit_solution(339420479612482489)
XLA Ops:
  0.0 23.0 %flow_variance_grad.1 = f32[64,512]{1,0:T(8,128)} custom-call(f32[64,512]{1,0:T(8,128)} %psi_hbm.1, f32[256,256]{1,0:T(8,128)} %lodf_hbm.1, s32[2,2]{1,0:T(2,128)} %map_hbm.1, f32[1,256]{1,0:T(1,128)} %bitcast.2, s32[1,256]{1,0:T(1,128)} %bitcast.3, s32[256]{0:T(256)} %outs_hbm.1), custom_call_target="tpu_custom_call" | custom-call | tf_op jit(solution)/shard_map/flow_variance_grad/pallas_call | solution.py:310
  23.0 1.6 %copy.8 = f32[64,512]{1,0:T(8,128)} copy(f32[64,512]{1,0:T(8,128)} %flow_variance_grad.1) | data formatting | bytes 262144

commit v3 on v2

--- a/solution.py
+++ b/solution.py
@@ -335,9 +335,9 @@
             dma((nz,)), dma((nz,)), dma((nz,)), dma((nz,)),
         ],
         compiler_params=pltpu.CompilerParams(
-            collective_id=0, has_side_effects=True, vmem_limit_bytes=60 << 20),
+            collective_id=0, has_side_effects=True, vmem_limit_bytes=40 << 20),
         name="flow_variance_grad",
-    )(psi, lodf, block_map, margin.reshape(1, -1), monitored.reshape(1, -1), outages)
+    )(*[pltpu.with_memory_space_constraint(x, pltpu.HBM) for x in (psi, lodf, block_map, margin.reshape(1, -1), monitored.reshape(1, -1), outages)])
 
 
 def solution(mesh):

time: 24.7 us -> 23.2 us (0.939)
  local copies, waits for them, and re-layouts: 1.57 us -> 0.66 us
  Pallas kernels: 23 us -> 22.4 us
    unnamed x1, local copies, waits for them, and re-layouts: 1.57 us -> 0.66 us
    pallas_call x1, Pallas kernels: 23 us -> 22.4 us  [body(): pl.pallas_call(functools.partial(kernel, n_mon, n_out, 2.0 / total_out),...]
where the time goes in v3:
time: 23.2 us; the launch traced here: 23 us
  Pallas kernels  22.4 us (97%)
  local copies, waits for them, and re-layouts  0.66 us (3%)
    pallas_call x1, Pallas kernels, body(): pl.pallas_call(functools.partial(kernel, n_mon, n_out, 2.0 / total_out),...  22.4 us
    unnamed x1, local copies, waits for them, and re-layouts  0.66 us

profile of v3, /device:TPU:0, one launch (start us, length us, event | category | flops | bytes accessed | tf_op | source)
XLA Modules:
  0.0 23.0 jit_solution(7027251442835500850)
XLA Ops:
  0.0 22.4 %flow_variance_grad.1 = f32[64,512]{1,0:T(8,128)S(1)} custom-call(f32[64,512]{1,0:T(8,128)} %psi_hbm.1, f32[256,256]{1,0:T(8,128)} %lodf_hbm.1, s32[2,2]{1,0:T(2,128)} %map_hbm.1, f32[1,256]{1,0:T(1,128)} %bitcast.2, s32[1,256]{1,0:T(1,128)} %bitcast.3, s32[256]{0:T(256)} %outs_hbm.1), custom_call_target="tpu_custom_call" | custom-call | tf_op jit(solution)/shard_map/flow_variance_grad/pallas_call | solution.py:310
  22.4 0.7 %copy.8 = f32[64,512]{1,0:T(8,128)} copy(f32[64,512]{1,0:T(8,128)S(1)} %flow_variance_grad.1) | data formatting | bytes 262144

commit v4 on v3

--- a/solution.py
+++ b/solution.py
@@ -32,7 +32,7 @@
            psi_hbm, lodf_hbm, map_hbm, margin_hbm, mon_hbm, outs_hbm,
            out_ref,
            lodf_ref, map_ref, margin_ref, mon_ref, outs_ref,
-           pv, pm, po, sel, selt, eff, marg, mpart, adj, rm, rs, rz,
+           pv, pm, po, sel, selt, eff, marg, mh, ml, own, mpart, adj, rm, rs, rz,
            loc_sem, sm_s, sm_r, so_s, so_r, fw_s, rl_s, bm_s, bm_r, bs_s, bs_r, bz_s, bz_r):
     nz = n_mon // 2
     i = lax.axis_index("mon")
@@ -58,6 +58,17 @@
     def from_z(d):
         return lax.rem(z + nz - d, nz)
 
+    def z_at(d):
+        if nz != 4:
+            return from_z(d + 1)
+        mid = (lax.rem(z, 3) + 1) // 2
+        near = (1 - mid) * (1 + z // 3) + mid * 3 * (z - 1)
+        if d == 0:
+            return near
+        if d == 1:
+            return (1 - mid) * (2 - z // 3) + mid * (3 - z)
+        return (1 - mid) * (3 - z) + mid * (3 - near)
+
     def loop(count, f):
         if count <= 8:
             for d in range(count):
@@ -68,19 +79,19 @@
     loads = [pltpu.make_async_copy(a, b, loc_sem.at[k]) for k, (a, b) in enumerate([
         (outs_hbm, outs_ref), (psi_hbm, pv), (mon_hbm, mon_ref),
         (margin_hbm, margin_ref), (map_hbm, map_ref), (lodf_hbm, lodf_ref)])]
+    barrier = pltpu.get_barrier_semaphore()
+
+    def sig_out(d):
+        pl.semaphore_signal(barrier, inc=1, device_id={"out": to_out(d + 1)}, device_id_type=MESH)
+
+    def sig_z(d):
+        pl.semaphore_signal(barrier, inc=1, device_id={"mon": 2 * to_z(d + 1) + c}, device_id_type=MESH)
+
+    loop(nz - 1, sig_z)
+    loop(n_out - 1, sig_out)
+    pl.semaphore_signal(barrier, inc=1, device_id={"mon": sib}, device_id_type=MESH)
     for load in loads:
         load.start()
-    barrier = pltpu.get_barrier_semaphore()
-
-    def sig_out(d):
-        pl.semaphore_signal(barrier, inc=1, device_id={"out": to_out(d + 1)}, device_id_type=MESH)
-
-    def sig_z(d):
-        pl.semaphore_signal(barrier, inc=1, device_id={"mon": 2 * to_z(d + 1) + c}, device_id_type=MESH)
-
-    loop(n_out - 1, sig_out)
-    loop(nz - 1, sig_z)
-    pl.semaphore_signal(barrier, inc=1, device_id={"mon": sib}, device_id_type=MESH)
     loads[0].wait()
     loads[1].wait()
     for k in range(SEL_O):
@@ -115,7 +126,7 @@
             device_id={"mon": sib}, device_id_type=MESH)
 
     def relay(d):
-        slot = 2 * from_z(d + 1) + c
+        slot = 2 * z_at(d) + c
         return pltpu.make_async_remote_copy(
             po.at[slot], po.at[slot], rl_s.at[d], so_r.at[slot],
             device_id={"mon": sib}, device_id_type=MESH)
@@ -164,18 +175,37 @@
         lax.fori_loop(0, chunks, lay, 0)
 
     def take_z(d):
-        slot = 2 * from_z(d + 1) + c
+        slot = 2 * z_at(d) + c
         from_slot(slot).wait_recv()
         relay(d).start()
 
-    loop(nz - 1, take_z)
-    loop(n_out - 1, lambda d: recv_m(d).wait_recv())
+    def prep(s):
+        block = pm[s]
+        hi, lo = split(block)
+        rows = pl.ds(pl.multiple_of(s * SEL_M, SEL_M), SEL_M)
+        mh[rows, :] = hi
+        ml[rows, :] = lo
+        own[rows, :] = jnp.sum(block * block, axis=1, keepdims=True) * (1.0 / width)
+
+    prep(j)
+    if nz <= 4:
+        for d in range(max(nz, n_out) - 1):
+            if d < nz - 1:
+                take_z(d)
+            if d < n_out - 1:
+                recv_m(d).wait_recv()
+                prep(from_out(d + 1))
+    else:
+        loop(nz - 1, take_z)
+        for d in range(n_out - 1):
+            recv_m(d).wait_recv()
+            prep(from_out(d + 1))
     from_slot(sib).wait_recv()
-    loop(nz - 1, lambda d: from_slot(2 * from_z(d + 1) + 1 - c).wait_recv())
+    loop(nz - 1, lambda d: from_slot(2 * z_at(d) + 1 - c).wait_recv())
 
     psi_m = pm[...].reshape(mon_count, width)
-    m2 = split(psi_m)
-    own_m = jnp.sum(psi_m * psi_m, axis=1, keepdims=True) * (1.0 / width)
+    m2 = (mh[...], ml[...])
+    own_m = own[...]
     margin = marg[...]
     ones_o = jnp.ones((8, width), BF16)
     ones_m = jnp.ones((mon_count, 128), BF16)
@@ -200,6 +230,17 @@
         q = inv * scale / (1.0 + jnp.exp(margin - 2.0 * (var1 * inv)))
         w = q * e
         w2 = split(w)
+        c2 = split(w * e)
+        dn0 = (((0,), (0,)), ((), ()))
+        colsum = (lax.dot_general(c2[0], ones_m, dn0, preferred_element_type=F32)
+                  + lax.dot_general(c2[1], ones_m, dn0, preferred_element_type=F32))[:, 0:1]
+        a = dot3(w2, m2, ((0,), (0,))) + colsum * psi_o
+        a = a.reshape(per, SEL_O, width)
+        for b in range(per):
+            adj[b % 2, ch * (per // 2) + b // 2] = a[b]
+        return q, w2, o2
+
+    def rows_part(ch, q, w2, o2):
         part = dot3(w2, o2, ((1,), (0,))) + jnp.sum(q, axis=1, keepdims=True) * psi_m
         part = part.reshape(n_out, SEL_M, width)
         if chunks == 1:
@@ -212,20 +253,6 @@
             @pl.when(ch > 0)
             def _():
                 mpart[...] += part
-        c2 = split(w * e)
-        dn0 = (((0,), (0,)), ((), ()))
-        colsum = (lax.dot_general(c2[0], ones_m, dn0, preferred_element_type=F32)
-                  + lax.dot_general(c2[1], ones_m, dn0, preferred_element_type=F32))[:, 0:1]
-        a = dot3(w2, m2, ((0,), (0,))) + colsum * psi_o
-        a = a.reshape(per, SEL_O, width)
-        for b in range(per):
-            adj[b % 2, ch * (per // 2) + b // 2] = a[b]
-        return 0
-
-    if chunks == 1:
-        compute(0, 0)
-    else:
-        lax.fori_loop(0, chunks, compute, 0)
 
     def sib_copy(d):
         zz = to_z(d)
@@ -257,7 +284,18 @@
             mpart.at[s], rm.at[s], bm_s.at[d], bm_r.at[s],
             device_id={"out": s}, device_id_type=MESH)
 
-    loop(nz, lambda d: sib_copy((d + 1) % nz if isinstance(d, int) else lax.rem(d + 1, nz)).start())
+    if chunks == 1:
+        mid = compute(0, 0)
+        for d in range(nz):
+            sib_copy((d + 1) % nz).start()
+        rows_part(0, *mid)
+    else:
+        def chunk(ch, _):
+            rows_part(ch, *compute(ch, 0))
+            return 0
+
+        lax.fori_loop(0, chunks, chunk, 0)
+        loop(nz, lambda d: sib_copy(lax.rem(d + 1, nz)).start())
     loop(n_out - 1, lambda d: b_copy(d).start())
 
     def pass_z(d):
@@ -325,6 +363,9 @@
             pltpu.VMEM((SEL_O, BR_DEV), F32),
             pltpu.VMEM((mon_count, out_count), F32),
             pltpu.VMEM((mon_count, 1), F32),
+            pltpu.VMEM((mon_count, width), BF16),
+            pltpu.VMEM((mon_count, width), BF16),
+            pltpu.VMEM((mon_count, 1), F32),
             pltpu.VMEM((n_out, BR_DEV, width), F32),
             pltpu.VMEM((2, nz, SEL_O, width), F32),
             pltpu.VMEM((n_out, BR_DEV, width), F32),

time: 23.2 us -> 23.7 us (1.022)
  Pallas kernels: 22.4 us -> 22.9 us
    pallas_call x1, Pallas kernels: 22.4 us -> 22.9 us  [body(): pl.pallas_call(functools.partial(kernel, n_mon, n_out, 2.0 / total_out),...]
where the time goes in v4:
time: 23.7 us; the launch traced here: 23.5 us
  Pallas kernels  22.9 us (97%)
  local copies, waits for them, and re-layouts  0.66 us (3%)
    pallas_call x1, Pallas kernels, body(): pl.pallas_call(functools.partial(kernel, n_mon, n_out, 2.0 / total_out),...  22.9 us
    unnamed x1, local copies, waits for them, and re-layouts  0.66 us

profile of v4, /device:TPU:0, one launch (start us, length us, event | category | flops | bytes accessed | tf_op | source)
XLA Modules:
  0.0 23.5 jit_solution(16521221802036374725)
XLA Ops:
  0.0 22.9 %flow_variance_grad.1 = f32[64,512]{1,0:T(8,128)S(1)} custom-call(f32[64,512]{1,0:T(8,128)} %psi_hbm.1, f32[256,256]{1,0:T(8,128)} %lodf_hbm.1, s32[2,2]{1,0:T(2,128)} %map_hbm.1, f32[1,256]{1,0:T(1,128)} %bitcast.2, s32[1,256]{1,0:T(1,128)} %bitcast.3, s32[256]{0:T(256)} %outs_hbm.1), custom_call_target="tpu_custom_call" | custom-call | tf_op jit(solution)/shard_map/flow_variance_grad/pallas_call | solution.py:348
  22.9 0.7 %copy.8 = f32[64,512]{1,0:T(8,128)} copy(f32[64,512]{1,0:T(8,128)S(1)} %flow_variance_grad.1) | data formatting | bytes 262144

commit v5 on v4

--- a/solution.py
+++ b/solution.py
@@ -32,7 +32,7 @@
            psi_hbm, lodf_hbm, map_hbm, margin_hbm, mon_hbm, outs_hbm,
            out_ref,
            lodf_ref, map_ref, margin_ref, mon_ref, outs_ref,
-           pv, pm, po, sel, selt, eff, marg, mh, ml, own, mpart, adj, rm, rs, rz,
+           pv, pm, po, sel, selt, eff, efft, marg, mpart, adj, rm, rs, rz,
            loc_sem, sm_s, sm_r, so_s, so_r, fw_s, rl_s, bm_s, bm_r, bs_s, bs_r, bz_s, bz_r):
     nz = n_mon // 2
     i = lax.axis_index("mon")
@@ -59,8 +59,7 @@
         return lax.rem(z + nz - d, nz)
 
     def z_at(d):
-        if nz != 4:
-            return from_z(d + 1)
+        return from_z(d + 1)
         mid = (lax.rem(z, 3) + 1) // 2
         near = (1 - mid) * (1 + z // 3) + mid * 3 * (z - 1)
         if d == 0:
@@ -166,7 +165,9 @@
         e1 = r1.astype(BF16)
         e2 = (r1 - e1.astype(F32)).astype(BF16)
         dot = functools.partial(jnp.dot, preferred_element_type=F32)
-        eff[:, cols] = dot(perm, e0) + (dot(perm, e1) + dot(perm, e2))
+        laid = dot(perm, e0) + (dot(perm, e1) + dot(perm, e2))
+        eff[:, cols] = laid
+        efft[cols, :] = laid.T
         return 0
 
     if chunks == 1:
@@ -179,36 +180,16 @@
         from_slot(slot).wait_recv()
         relay(d).start()
 
-    def prep(s):
-        block = pm[s]
-        hi, lo = split(block)
-        rows = pl.ds(pl.multiple_of(s * SEL_M, SEL_M), SEL_M)
-        mh[rows, :] = hi
-        ml[rows, :] = lo
-        own[rows, :] = jnp.sum(block * block, axis=1, keepdims=True) * (1.0 / width)
-
-    prep(j)
-    if nz <= 4:
-        for d in range(max(nz, n_out) - 1):
-            if d < nz - 1:
-                take_z(d)
-            if d < n_out - 1:
-                recv_m(d).wait_recv()
-                prep(from_out(d + 1))
-    else:
-        loop(nz - 1, take_z)
-        for d in range(n_out - 1):
-            recv_m(d).wait_recv()
-            prep(from_out(d + 1))
+    loop(nz - 1, take_z)
+    loop(n_out - 1, lambda d: recv_m(d).wait_recv())
     from_slot(sib).wait_recv()
     loop(nz - 1, lambda d: from_slot(2 * z_at(d) + 1 - c).wait_recv())
 
     psi_m = pm[...].reshape(mon_count, width)
-    m2 = (mh[...], ml[...])
-    own_m = own[...]
+    m2 = split(psi_m)
+    own_m = jnp.sum(psi_m * psi_m, axis=1, keepdims=True) * (1.0 / width)
     margin = marg[...]
     ones_o = jnp.ones((8, width), BF16)
-    ones_m = jnp.ones((mon_count, 128), BF16)
 
     def compute(ch, _):
         if chunks == 1:
@@ -230,11 +211,9 @@
         q = inv * scale / (1.0 + jnp.exp(margin - 2.0 * (var1 * inv)))
         w = q * e
         w2 = split(w)
-        c2 = split(w * e)
-        dn0 = (((0,), (0,)), ((), ()))
-        colsum = (lax.dot_general(c2[0], ones_m, dn0, preferred_element_type=F32)
-                  + lax.dot_general(c2[1], ones_m, dn0, preferred_element_type=F32))[:, 0:1]
-        a = dot3(w2, m2, ((0,), (0,))) + colsum * psi_o
+        wt = w.T
+        colsum = jnp.sum(wt * efft[cols, :], axis=1, keepdims=True)
+        a = dot3(split(wt), m2, ((1,), (0,))) + colsum * psi_o
         a = a.reshape(per, SEL_O, width)
         for b in range(per):
             adj[b % 2, ch * (per // 2) + b // 2] = a[b]
@@ -362,9 +341,7 @@
             pltpu.VMEM((SEL_O, width), F32),
             pltpu.VMEM((SEL_O, BR_DEV), F32),
             pltpu.VMEM((mon_count, out_count), F32),
-            pltpu.VMEM((mon_count, 1), F32),
-            pltpu.VMEM((mon_count, width), BF16),
-            pltpu.VMEM((mon_count, width), BF16),
+            pltpu.VMEM((out_count, mon_count), F32),
             pltpu.VMEM((mon_count, 1), F32),
             pltpu.VMEM((n_out, BR_DEV, width), F32),
             pltpu.VMEM((2, nz, SEL_O, width), F32),

time: 23.7 us -> 23 us (0.970)
  Pallas kernels: 22.9 us -> 22.2 us
    pallas_call x1, Pallas kernels: 22.9 us -> 22.2 us  [body(): pl.pallas_call(functools.partial(kernel, n_mon, n_out, 2.0 / total_out),...]
where the time goes in v5:
time: 23 us; the launch traced here: 22.8 us
  Pallas kernels  22.2 us (97%)
  local copies, waits for them, and re-layouts  0.66 us (3%)
    pallas_call x1, Pallas kernels, body(): pl.pallas_call(functools.partial(kernel, n_mon, n_out, 2.0 / total_out),...  22.2 us
    unnamed x1, local copies, waits for them, and re-layouts  0.66 us

profile of v5, /device:TPU:0, one launch (start us, length us, event | category | flops | bytes accessed | tf_op | source)
XLA Modules:
  0.0 22.8 jit_solution(451799953655695710)
XLA Ops:
  0.0 22.2 %flow_variance_grad.1 = f32[64,512]{1,0:T(8,128)S(1)} custom-call(f32[64,512]{1,0:T(8,128)} %psi_hbm.1, f32[256,256]{1,0:T(8,128)} %lodf_hbm.1, s32[2,2]{1,0:T(2,128)} %map_hbm.1, f32[1,256]{1,0:T(1,128)} %bitcast.2, s32[1,256]{1,0:T(1,128)} %bitcast.3, s32[256]{0:T(256)} %outs_hbm.1), custom_call_target="tpu_custom_call" | custom-call | tf_op jit(solution)/shard_map/flow_variance_grad/pallas_call | solution.py:327
  22.2 0.7 %copy.8 = f32[64,512]{1,0:T(8,128)} copy(f32[64,512]{1,0:T(8,128)S(1)} %flow_variance_grad.1) | data formatting | bytes 262144

commit v6 on v5

--- a/solution.py
+++ b/solution.py
@@ -32,7 +32,7 @@
            psi_hbm, lodf_hbm, map_hbm, margin_hbm, mon_hbm, outs_hbm,
            out_ref,
            lodf_ref, map_ref, margin_ref, mon_ref, outs_ref,
-           pv, pm, po, sel, selt, eff, efft, marg, mpart, adj, rm, rs, rz,
+           pv, pm, po, sel, selt, eff, efft, marg, mh, ml, own, mpart, adj, rm, rs, rz,
            loc_sem, sm_s, sm_r, so_s, so_r, fw_s, rl_s, bm_s, bm_r, bs_s, bs_r, bz_s, bz_r):
     nz = n_mon // 2
     i = lax.axis_index("mon")
@@ -58,16 +58,6 @@
     def from_z(d):
         return lax.rem(z + nz - d, nz)
 
-    def z_at(d):
-        return from_z(d + 1)
-        mid = (lax.rem(z, 3) + 1) // 2
-        near = (1 - mid) * (1 + z // 3) + mid * 3 * (z - 1)
-        if d == 0:
-            return near
-        if d == 1:
-            return (1 - mid) * (2 - z // 3) + mid * (3 - z)
-        return (1 - mid) * (3 - z) + mid * (3 - near)
-
     def loop(count, f):
         if count <= 8:
             for d in range(count):
@@ -125,7 +115,7 @@
             device_id={"mon": sib}, device_id_type=MESH)
 
     def relay(d):
-        slot = 2 * z_at(d) + c
+        slot = 2 * from_z(d + 1) + c
         return pltpu.make_async_remote_copy(
             po.at[slot], po.at[slot], rl_s.at[d], so_r.at[slot],
             device_id={"mon": sib}, device_id_type=MESH)
@@ -176,18 +166,23 @@
         lax.fori_loop(0, chunks, lay, 0)
 
     def take_z(d):
-        slot = 2 * z_at(d) + c
+        slot = 2 * from_z(d + 1) + c
         from_slot(slot).wait_recv()
         relay(d).start()
 
     loop(nz - 1, take_z)
     loop(n_out - 1, lambda d: recv_m(d).wait_recv())
+    block = pm[...].reshape(mon_count, width)
+    hi, lo = split(block)
+    mh[...] = hi
+    ml[...] = lo
+    own[...] = jnp.sum(block * block, axis=1, keepdims=True) * (1.0 / width)
     from_slot(sib).wait_recv()
-    loop(nz - 1, lambda d: from_slot(2 * z_at(d) + 1 - c).wait_recv())
+    loop(nz - 1, lambda d: from_slot(2 * from_z(d + 1) + 1 - c).wait_recv())
 
     psi_m = pm[...].reshape(mon_count, width)
-    m2 = split(psi_m)
-    own_m = jnp.sum(psi_m * psi_m, axis=1, keepdims=True) * (1.0 / width)
+    m2 = (mh[...], ml[...])
+    own_m = own[...]
     margin = marg[...]
     ones_o = jnp.ones((8, width), BF16)
 
@@ -343,6 +338,9 @@
             pltpu.VMEM((mon_count, out_count), F32),
             pltpu.VMEM((out_count, mon_count), F32),
             pltpu.VMEM((mon_count, 1), F32),
+            pltpu.VMEM((mon_count, width), BF16),
+            pltpu.VMEM((mon_count, width), BF16),
+            pltpu.VMEM((mon_count, 1), F32),
             pltpu.VMEM((n_out, BR_DEV, width), F32),
             pltpu.VMEM((2, nz, SEL_O, width), F32),
             pltpu.VMEM((n_out, BR_DEV, width), F32),

time: 23 us -> 23.1 us (level)
  no operation moved by 1% of the time
where the time goes in v6:
time: 23.1 us; the launch traced here: 23 us
  Pallas kernels  22.3 us (97%)
  local copies, waits for them, and re-layouts  0.66 us (3%)
    pallas_call x1, Pallas kernels, body(): pl.pallas_call(functools.partial(kernel, n_mon, n_out, 2.0 / total_out),...  22.3 us
    unnamed x1, local copies, waits for them, and re-layouts  0.66 us

profile of v6, /device:TPU:0, one launch (start us, length us, event | category | flops | bytes accessed | tf_op | source)
XLA Modules:
  0.0 23.0 jit_solution(11183021460407605363)
XLA Ops:
  0.0 22.3 %flow_variance_grad.1 = f32[64,512]{1,0:T(8,128)S(1)} custom-call(f32[64,512]{1,0:T(8,128)} %psi_hbm.1, f32[256,256]{1,0:T(8,128)} %lodf_hbm.1, s32[2,2]{1,0:T(2,128)} %map_hbm.1, f32[1,256]{1,0:T(1,128)} %bitcast.2, s32[1,256]{1,0:T(1,128)} %bitcast.3, s32[256]{0:T(256)} %outs_hbm.1), custom_call_target="tpu_custom_call" | custom-call | tf_op jit(solution)/shard_map/flow_variance_grad/pallas_call | solution.py:322
  22.3 0.7 %copy.8 = f32[64,512]{1,0:T(8,128)} copy(f32[64,512]{1,0:T(8,128)S(1)} %flow_variance_grad.1) | data formatting | bytes 262144
